TPU v7x, 256 devices: a whole 4x4x8 slice. The times are simulated.
256 devices in a mesh: ctx: 32 (over x, z), head: 8 (over y, core).
Axes of the slice: x: 4, y: 4, z: 8, core: 2. Of those that a mesh axis runs over, the one named last changes fastest.
Arguments:
- ssm_input: bfloat16 [8192, 8192], P('ctx', 'head'), may hold values from -6 to 6
- gate_input: bfloat16 [8192, 8192], P('ctx', 'head'), may hold values from -6 to 6
- in_state: bfloat16 [8192, 1024], P('ctx', 'head'), may hold values from -0.5 to 0.5
- out_state: bfloat16 [8192, 1024], P('ctx', 'head'), may hold values from -0.5 to 0.5
- step_size: float32 [8192, 128], P('ctx', 'head'), may hold values from 0.05 to 0.5
- log_decay: float32 [8192, 128], P('ctx', 'head'), may hold values from 0 to 2
- skip_gain: float32 [128], P('head'), may hold values from 0.5 to 1.5
- norm_gain: float32 [8192], P('head'), may hold values from 0.5 to 1.5
- queries: bfloat16 [8192, 8192], P('ctx', 'head'), may hold values from -5 to 5
- keys: bfloat16 [8192, 1024], P('ctx', 'head'), may hold values from -5 to 5
- values: bfloat16 [8192, 1024], P('ctx', 'head'), may hold values from -6 to 6
Outputs:
- mamba_out: bfloat16 [8192, 8192], P('ctx', 'head')
- attention_out: bfloat16 [8192, 8192], P('ctx', 'head')
All inputs are finite; a program needn't handle non-finite values.
Results may differ from a plain program's by a relative error of at most 0.014.
Values may be sent and summed in bfloat16 or wider, within the bound.
No kernel may reach another device: no remote copies, remote signals or barrier semaphores. Data moves between devices by JAX's collectives and lax.ppermute only.
A program may use at most 128 MiB of HBM per device.

v0:
```python
import jax
import jax.numpy as jnp
from jax import lax
from jax.sharding import PartitionSpec as P

MIXER_HEADS = 128
P_SIZE = 64
N = 128
HQ = 64
KVH = 8
DH = 128
BLOCK = 256


HIGH = lax.Precision.HIGHEST


def carried_in(value, axis, join, neutral):
    place = lax.axis_index(axis)
    gathered = jax.tree.map(
        lambda a, kind: lax.all_gather(a.astype(kind), axis), value, (jnp.bfloat16, jnp.bfloat16)
    )
    state = jax.tree.map(lambda a, e: jnp.zeros_like(a) + jnp.asarray(e, a.dtype), value, neutral)

    def one(turn, state):
        return join(
            state,
            jax.tree.map(
                lambda a, own: lax.dynamic_index_in_dim(a, turn, 0, False).astype(own.dtype),
                gathered,
                value,
            ),
        )

    return lax.fori_loop(0, place, one, state)


def block_segments(signal, enter, enter_half, leave_half, step_size, decay):
    length = signal.shape[0]
    running_state = jnp.cumsum(decay, axis=0)
    scaled = signal * step_size[..., None]
    affinity = jnp.einsum(
        "tgn,sgn->tsg", leave_half, enter_half, preferred_element_type=jnp.float32
    )
    order = jnp.arange(length, dtype=jnp.int32)
    causal = (order[:, None] >= order[None, :])[:, :, None, None]
    spread = jnp.where(causal, running_state[:, None] - running_state[None, :], 0.0)
    mixing = jnp.where(causal, jnp.exp(-spread), 0.0) * affinity[..., None]
    within_block = jnp.einsum("tsgk,sgkp->tgkp", mixing, scaled, precision=HIGH)
    total_sum = running_state[-1]
    remain = jnp.exp(running_state - total_sum[None])
    state_contribution = jnp.einsum(
        "sgn,sgkp->gknp", enter, scaled * remain[..., None], precision=HIGH
    )
    return (within_block, state_contribution, jnp.exp(-total_sum), running_state, total_sum)


def past_carryover(leave, running_state, state_matrix):
    return (
        jnp.einsum("tgn,gknp->tgkp", leave, state_matrix, precision=HIGH)
        * jnp.exp(-running_state)[..., None]
    )


def mamba_mixer(
    ssm_input, gate_input, in_state, out_state, step_size, log_decay, skip_gain, norm_gain
):
    tokens_here = ssm_input.shape[0]
    count = tokens_here // BLOCK
    heads_here = skip_gain.shape[0]
    groups_here = in_state.shape[1] // N
    per_group = heads_here // groups_here
    signal = ssm_input.astype(jnp.float32).reshape(count, BLOCK, groups_here, per_group, P_SIZE)
    enter_half = in_state.reshape(count, BLOCK, groups_here, N)
    leave_half = out_state.reshape(count, BLOCK, groups_here, N)
    enter = enter_half.astype(jnp.float32)
    leave = leave_half.astype(jnp.float32)
    stepped = step_size.reshape(count, BLOCK, groups_here, per_group)
    decay = log_decay.reshape(count, BLOCK, groups_here, per_group)
    skip_path = skip_gain.reshape(groups_here, per_group)
    pieces = block_segments(signal[0], enter[0], enter_half[0], leave_half[0], stepped[0], decay[0])
    fade_all = jnp.ones((groups_here, per_group), jnp.float32)
    carried = jnp.zeros((groups_here, per_group, N, P_SIZE), jnp.float32)
    carried = pieces[2][..., None, None] * carried + pieces[1]
    fade_all = fade_all * pieces[2]

    def combine(earlier, later):
        return (earlier[0] * later[0], later[0][..., None, None] * earlier[1] + later[1])

    identity = (jnp.ones_like(fade_all), jnp.zeros_like(carried))
    _, state_matrix = carried_in((fade_all, carried), "ctx", combine, identity)
    within_block, state_contribution, fading_factor, running_state, total_sum = pieces
    mixed_output = (
        within_block
        + past_carryover(leave[0], running_state, state_matrix)
        + skip_path[..., None] * signal[0]
    )
    outputs = [mixed_output]
    mixed_output = jnp.stack(outputs).reshape(tokens_here, heads_here * P_SIZE)
    gated = mixed_output * jax.nn.silu(gate_input.astype(jnp.float32))
    squares = lax.psum(jnp.sum(gated * gated, axis=1), "head")
    scale = lax.rsqrt(squares / (MIXER_HEADS * P_SIZE) + 1e-05)
    return (gated * scale[:, None] * norm_gain).astype(jnp.bfloat16)


def attention(queries, keys, values):
    tokens_here = queries.shape[0]
    kv_here = keys.shape[1] // DH
    per_kv = HQ // KVH
    query_rows = queries.reshape(tokens_here, kv_here, per_kv, DH)
    first = lax.axis_index("ctx") * tokens_here
    query_pos = first + jnp.arange(tokens_here, dtype=jnp.int32)
    factor = DH ** (-0.5)

    def update(carry, key_block, value_block, key_pos):
        peak, total_sum, summed = carry
        score = (
            jnp.einsum("tgqd,jgd->gqtj", query_rows, key_block, preferred_element_type=jnp.float32)
            * factor
        )
        mask = (key_pos[None, :] <= query_pos[:, None])[None, None]
        block_peak = jnp.max(jnp.where(mask, score, -1e30), axis=-1)
        new_peak = jnp.maximum(peak, block_peak)
        weight = jnp.where(mask, jnp.exp(score - new_peak[..., None]), 0.0)
        shrink = jnp.exp(peak - new_peak)
        total_sum = total_sum * shrink + jnp.sum(weight, axis=-1)
        summed = summed * shrink[..., None] + jnp.einsum(
            "gqtj,jgd->gqtd",
            weight.astype(jnp.bfloat16),
            value_block,
            preferred_element_type=jnp.float32,
        )
        return (new_peak, total_sum, summed)

    initial = (
        jnp.full((kv_here, per_kv, tokens_here), -1e30, jnp.float32),
        jnp.zeros((kv_here, per_kv, tokens_here), jnp.float32),
        jnp.zeros((kv_here, per_kv, tokens_here, DH), jnp.float32),
    )
    carry = initial
    key_piece = lax.all_gather(keys, "ctx", axis=0, tiled=True)
    value_piece = lax.all_gather(values, "ctx", axis=0, tiled=True)
    rows = key_piece.shape[0]
    width = 512
    number = rows // width
    key_blocks = key_piece.reshape(number, width, kv_here, DH)
    value_blocks = value_piece.reshape(number, width, kv_here, DH)

    def advance(inner, block_slice):
        key_block, value_block, index = block_slice
        block_start = index * width
        key_pos = block_start + jnp.arange(width, dtype=jnp.int32)
        inner = update(inner, key_block, value_block, key_pos)
        return (inner, None)

    carry, _ = lax.scan(
        advance, carry, (key_blocks, value_blocks, jnp.arange(number, dtype=jnp.int32))
    )
    peak, total_sum, summed = carry
    result = summed / total_sum[..., None]
    result = jnp.transpose(result, (2, 0, 1, 3)).reshape(tokens_here, kv_here * per_kv * DH)
    return result.astype(jnp.bfloat16)


def per_device(
    ssm_input,
    gate_input,
    in_state,
    out_state,
    step_size,
    log_decay,
    skip_gain,
    norm_gain,
    queries,
    keys,
    values,
):
    mamba_out = mamba_mixer(
        ssm_input, gate_input, in_state, out_state, step_size, log_decay, skip_gain, norm_gain
    )
    attention_out = attention(queries, keys, values)
    return (mamba_out, attention_out)


def solution(mesh):
    return jax.shard_map(
        per_device,
        mesh=mesh,
        in_specs=(
            P("ctx", "head"),
            P("ctx", "head"),
            P("ctx", "head"),
            P("ctx", "head"),
            P("ctx", "head"),
            P("ctx", "head"),
            P("head"),
            P("head"),
            P("ctx", "head"),
            P("ctx", "head"),
            P("ctx", "head"),
        ),
        out_specs=(P("ctx", "head"), P("ctx", "head")),
        check_vma=False,
    )
```

profile of v0, /device:TPU:231, one launch (start us, length us, event | category | flops | bytes accessed | tf_op | source)
XLA Modules:
  0.0 396.7 jit_solution(6865414195518606855)
XLA Ops:
  15.9 28.9 %all_gather.16 = bf16[32,1,16]{2,1,0:T(2,128)(2,1)S(1)} all-gather(bf16[1,1,16]{2,1,0:T(2,128)(2,1)S(1)} %get-tuple-element.226), channel_id=1, replica_groups=mesh['ctx'=32,'head'=8] {'ctx'}, dimensions={0}, use_global_device_ids=true | all-gather | bytes 1056 | tf_op jit(solution)/shard_map/all_gather | solution.py:21
  46.8 6.7 %fusion.40 = f32[256,1,16,64]{0,3,2,1:T(8,128)} fusion(f32[256,256]{1,0:T(8,128)S(1)} %copy.73, f32[256,16]{0,1:T(8,128)S(1)} %copy.71, pred[256,256]{1,0:T(8,128)(4,1)} %iota_compare_fusion, f32[256,16,64]{0,2,1:T(8,128)S(1)} %bitcast.182, f32[256,16]{0,1:T(8,128)S(1)} %copy-done.3), kind=kOutput, calls=%fused_computation.47 | convolution fusion | flops 810811392 | bytes 2457600 | tf_op jit(solution)/shard_map/tsgk,sgkp->tgkp/dot_general | solution.py:49
  53.5 28.7 %all-gather.5.cloned.1.call-done = bf16[8192,128]{1,0:T(8,128)(2,1)} async-done(((bf16[256,128]{1,0:T(8,128)(2,1)}), bf16[8192,128]{1,0:T(8,128)(2,1)}) %all-gather.5.cloned.1.call-update) | async-done | bytes 2097168 | tf_op jit(solution)/shard_map/all_gather | solution.py:141
  82.3 77.7 %all-gather.7.cloned.1.call-done = bf16[8192,128]{1,0:T(8,128)(2,1)} async-done(((bf16[256,128]{1,0:T(8,128)(2,1)}), bf16[8192,128]{1,0:T(8,128)(2,1)}) %all-gather.7.cloned.1.call-update) | async-done | bytes 2097168 | tf_op jit(solution)/shard_map/all_gather | solution.py:142
  160.0 157.5 %while.28 = (s32[]{:T(128)}, f32[1,8,256]{2,1,0:T(8,128)S(1)}, f32[1,8,256]{2,1,0:T(8,128)S(1)}, f32[1,8,256,128]{3,2,1,0:T(8,128)S(1)}, s32[16]{0:T(128)S(1)}, ...) while((s32[]{:T(128)}, f32[1,8,256]{2,1,0:T(8,128)S(1)}, ...), condition=%wide.region_9.10_spmd.clone, body=%wide.region_6.9_spmd.clone.sunk | while | flops 549335808 | bytes 32906428 | solution.py:156
  161.4 3.7 fusion.72
  165.1 3.8 fusion.75
  174.9 3.8 fusion.75
  184.7 3.8 fusion.75
  194.6 3.8 fusion.75
  204.4 3.8 fusion.75
  214.3 3.8 fusion.75
  224.1 3.9 fusion.75
  234.0 3.9 fusion.75
  243.9 3.8 fusion.75
  253.8 3.8 fusion.75
  263.6 3.8 fusion.75
  273.5 3.8 fusion.75
  283.3 3.8 fusion.75
  293.1 3.8 fusion.75
  302.9 3.8 fusion.75
  312.8 3.8 fusion.75
  319.2 48.5 %while.27 = (s32[]{:T(128)}, f32[1,16,128,64]{3,2,1,0:T(8,128)S(1)}, s32[]{:T(128)}, bf16[32,1,16]{2,1,0:T(2,128)(2,1)S(1)}, bf16[32,1,16,128,64]{3,4,2,0,1:T(8,128)(2,1)}, /*index=5*/s32[]{:T(128)}, s32[]{:T(128)}, s32[]{:T(128)}) while((s32[]{:T(128)}, f32[1,16,128,64]{3,2,1,0:T(8,128)S(1)}, s32[]{:T(128)}, ...), condition=%wide.region_3.4_spmd, body=%wide.region_2.3_spmd.sunk | while | flops 393237 | bytes 2359583 | solution.py:35
  371.8 16.2 %psum.7 = f32[256]{0:T(256)S(1)} all-reduce(f32[256]{0:T(256)S(1)} %multiply_reduce_fusion), channel_id=1, replica_groups=mesh['ctx'=32,'head'=8] {'head'}, use_global_device_ids=true, to_apply=%region_5.6 | all-reduce | flops 256 | bytes 2048 | tf_op jit(solution)/shard_map/psum | solution.py:101
  (353 shorter events, 146.9 us)
Async XLA Ops:
  7.2 37.7 %copy-start = (bf16[256,128]{1,0:T(8,128)(2,1)S(1)}, bf16[256,128]{1,0:T(8,128)(2,1)}, u32[]{:S(2)}) copy-start(bf16[256,128]{1,0:T(8,128)(2,1)} %param.18) | copy-start | bytes 196612
  7.2 37.7 %copy-start.2 = (bf16[256,128]{1,0:T(8,128)(2,1)S(1)}, bf16[256,128]{1,0:T(8,128)(2,1)}, u32[]{:S(2)}) copy-start(bf16[256,128]{1,0:T(8,128)(2,1)} %param.17) | copy-start | bytes 196612
  7.2 75.1 %all-gather.5.cloned.1.call-start = ((), (), s32[]{:S(2)}) async-start(), calls=%async_computation | async-start | bytes 2162688 | tf_op jit(solution)/shard_map/all_gather | solution.py:141
  7.9 152.1 %all-gather.7.cloned.1.call-start = ((), (), s32[]{:S(2)}) async-start(), calls=%async_computation.1 | async-start | bytes 2162688 | tf_op jit(solution)/shard_map/all_gather | solution.py:142
  8.7 310.4 %all-gather.9.cloned.1.call-start = ((), (), s32[]{:S(2)}) async-start(), calls=%async_computation.2 | async-start | bytes 8650752 | tf_op jit(solution)/shard_map/all_gather | solution.py:21
  12.1 34.8 %copy-start.3 = (f32[256,16]{0,1:T(8,128)S(1)}, f32[256,16]{0,1:T(8,128)}, u32[]{:S(2)}) copy-start(f32[256,16]{0,1:T(8,128)} %param.19) | copy-start | bytes 49156
  165.1 3.8 copy-start.1
  174.9 3.8 copy-start.1
  184.7 3.8 copy-start.1
  194.6 3.8 copy-start.1
  204.4 3.8 copy-start.1
  214.2 3.8 copy-start.1
  224.1 3.9 copy-start.1
  234.0 4.0 copy-start.1
  243.9 3.8 copy-start.1
  253.8 3.9 copy-start.1
  263.6 3.8 copy-start.1
  273.5 3.8 copy-start.1
  283.3 3.8 copy-start.1
  293.1 3.8 copy-start.1
  302.9 3.8 copy-start.1
  312.7 3.8 copy-start.1
  319.2 48.5 %copy-start.5 = (f32[16]{0:T(128)S(1)}, f32[16]{0:T(128)}, u32[]{:S(2)}) copy-start(f32[16]{0:T(128)} %param.21) | copy-start | bytes 196
  367.7 20.3 %copy-start.4 = (f32[1024]{0:T(1024)S(1)}, f32[1024]{0:T(1024)}, u32[]{:S(2)}) copy-start(f32[1024]{0:T(1024)} %param.22) | copy-start | bytes 12292
Sparse Core Ops, SparseCore 0:
  10.6 71.6 all-gather.4
  84.9 75.1 all-gather.6
  163.2 97.9 all-gather.8
where the time goes:
time: 399 us; the launch traced here: 397 us
  matrix products  131 us (33%)
  waiting for transfers between devices  108 us (27%)
  local copies, waits for them, and re-layouts  54.3 us (14%)
  blocking collectives  45.1 us (11%)
  other arithmetic  31.6 us (8%)
  between operations  13.9 us (3%)
  loops' own time  12.9 us (3%)
    all_gather x1, waiting for transfers between devices, attention(): value_piece = lax.all_gather(values, 'ctx', axis=0, tiled=True)  77.7 us
    dot_general x16, matrix products, update(): jnp.einsum('gqtj,jgd->gqtd', weight.astype(jnp.bfloat16), value_block, pr...  61 us
    dot_general x16, matrix products, update(): jnp.einsum('tgqd,jgd->gqtj', query_rows, key_block, preferred_element_typ...  58.5 us
    dynamic_slice x62, local copies, waits for them, and re-layouts, one(): lax.dynamic_index_in_dim(a, turn, 0, False).astype(own.dtype)  39 us
    all_gather x1, blocking collectives, carried_in(): lax.all_gather(a.astype(kind), axis)  28.9 us
    all_gather x1, waiting for transfers between devices, attention(): key_piece = lax.all_gather(keys, 'ctx', axis=0, tiled=True)  28.7 us
    psum x1, blocking collectives, mamba_mixer(): squares = lax.psum(jnp.sum(gated * gated, axis=1), 'head')  16.2 us
    reduce_sum x16, other arithmetic, update(): total_sum = total_sum * shrink + jnp.sum(weight, axis=-1)  14.1 us
  transfers between devices with their start and end apart: 3, of which 2 were waited for; matrix products, arithmetic and copies ran while one was open for 41% of the time, Pallas kernels for 0%

commit v1 on v0

v1 whole, which is shorter than its diff:
```python
import functools
import math

import jax
import jax.numpy as jnp
from jax import lax
from jax.experimental import pallas as pl
from jax.experimental.pallas import tpu as pltpu
from jax.sharding import PartitionSpec as P

MIXER_HEADS = 128
P_SIZE = 64
DH = 128
BLOCK = 256
XS = 4
ZS = 8
CTX = XS * ZS
HEADS = 16
WIDTH = HEADS * P_SIZE
LOG2E = math.log2(math.e)
SCALE = LOG2E * DH ** (-0.5)
F32 = jnp.float32
BF16 = jnp.bfloat16
HIGH = lax.Precision.HIGHEST
NT = (((1,), (1,)), ((), ()))
TN = (((0,), (0,)), ((), ()))


def dot(a, b, dims=(((1,), (0,)), ((), ())), precision=None):
    return lax.dot_general(a, b, dims, precision=precision, preferred_element_type=F32)


def halves(v):
    high = v.astype(BF16)
    return high, (v - high.astype(F32)).astype(BF16)


def spread_heads(v):
    lane = lax.broadcasted_iota(jnp.int32, (HEADS, WIDTH), 1)
    head = lax.broadcasted_iota(jnp.int32, (HEADS, WIDTH), 0)
    expand = jnp.where((lane >> 6) == head, 1.0, 0.0).astype(BF16)
    high, low = halves(v)
    return dot(high, expand) + dot(low, expand)


def local_kernel(x_ref, b_ref, c_ref, dt_ref, a_ref, skip_ref, y_ref, msg_ref, ec_ref):
    row = lax.broadcasted_iota(jnp.int32, (BLOCK, BLOCK), 0)
    col = lax.broadcasted_iota(jnp.int32, (BLOCK, BLOCK), 1)
    causal = col <= row
    a = a_ref[...]
    dt = dt_ref[...]
    cum = dot(jnp.where(causal, 1.0, 0.0), a, precision=HIGH)
    cum_rows = dot(a, jnp.where(row <= col, 1.0, 0.0), TN, precision=HIGH)
    last = cum[BLOCK - 1 :, :]
    ec_ref[...] = jnp.exp(-cum)
    x = x_ref[...].astype(F32)
    xs = (x * spread_heads(dt)).astype(BF16)
    xr = (x * spread_heads(dt * jnp.exp(cum - last))).astype(BF16)
    skip = spread_heads(jnp.broadcast_to(skip_ref[...], (8, HEADS)))[:1]
    fade = spread_heads(jnp.broadcast_to(jnp.exp(-last), (8, HEADS)))
    fade_high, fade_low = halves(fade)
    contrib = dot(b_ref[...], xr, TN).astype(BF16)
    for q in range(HEADS // 2):
        lanes = slice(q * 128, (q + 1) * 128)
        tail = jnp.concatenate([fade_high[:, lanes], fade_low[:, lanes]], axis=0)
        for r in range(4):
            msg_ref[q * 4 + r, 0:32, :] = contrib[r * 32 : (r + 1) * 32, lanes]
            msg_ref[q * 4 + r, 32:48, :] = tail
    affinity = jnp.where(causal, dot(c_ref[...], b_ref[...], NT), 0.0)
    cum2 = cum * LOG2E
    cum2_rows = cum_rows * LOG2E
    half = BLOCK // 2
    low_lane = lax.broadcasted_iota(jnp.int32, (BLOCK, 128), 1) < P_SIZE
    for q in range(HEADS // 2):
        lanes = slice(q * 128, (q + 1) * 128)
        xp = xs[:, lanes]
        parts = []
        for h in (2 * q, 2 * q + 1):
            across = cum2_rows[h : h + 1, :]
            down = cum2[:, h : h + 1]
            top = jnp.exp2(jnp.minimum(across[:, :half] - down[:half], 0.0)) * affinity[:half, :half]
            low = jnp.exp2(jnp.minimum(across - down[half:], 0.0)) * affinity[half:, :]
            parts.append(
                jnp.concatenate([dot(top.astype(BF16), xp[:half]), dot(low.astype(BF16), xp)], axis=0)
            )
        y_ref[:, lanes] = jnp.where(low_lane, parts[0], parts[1]) + skip[:, lanes] * x[:, lanes]


def scan_kernel(msg_ref, out_ref):
    state = jnp.zeros((32, 128), F32)
    for i in range(CTX):
        out_ref[i] = state.astype(BF16)
        piece = msg_ref[i].astype(F32)
        fade = piece[32:33] + piece[40:41]
        state = fade * state + piece[:32]


def gate_kernel(y_ref, c_ref, st_ref, ec_ref, z_ref, g_ref, ss_ref):
    ec = spread_heads(ec_ref[...])
    c = c_ref[...]
    total = jnp.zeros((BLOCK, 128), F32)
    for q in range(HEADS // 2):
        lanes = slice(q * 128, (q + 1) * 128)
        mixed = y_ref[:, lanes] + dot(c, st_ref[q]) * ec[:, lanes]
        z = z_ref[:, lanes].astype(F32)
        gated = mixed * (z / (1.0 + jnp.exp(-z)))
        g_ref[:, lanes] = gated
        total = total + gated * gated
    high, low = halves(total)
    ones = jnp.ones((8, 128), BF16)
    ss_ref[...] = dot(ones, high, NT) + dot(ones, low, NT)


def norm_kernel(g_ref, ss_ref, gain_ref, out_ref):
    total = dot(ss_ref[...], jnp.ones((8, 128), F32), TN, precision=HIGH)
    scale = lax.rsqrt(total * (1.0 / (MIXER_HEADS * P_SIZE)) + 1e-05)
    for q in range(HEADS // 2):
        lanes = slice(q * 128, (q + 1) * 128)
        out_ref[:, lanes] = (g_ref[:, lanes] * scale * gain_ref[:, lanes]).astype(BF16)


def attend_kernel(counts, first, last, flags, *refs):
    n = len(counts)
    q_ref, kv_refs = refs[0], refs[1 : 1 + n]
    refs = refs[1 + n :]
    if not first:
        m_in, l_in, acc_in = refs[:3]
        refs = refs[3:]
    if last:
        out_ref, m_ref, l_ref, acc_ref = refs
    else:
        m_ref, l_ref, acc_ref = refs
    if first:
        m_ref[...] = jnp.full((BLOCK, DH), -1e30, F32)
        l_ref[...] = jnp.zeros((BLOCK, DH), F32)
        acc_ref[...] = jnp.zeros((BLOCK, DH), F32)
    else:
        m_ref[...] = m_in[...]
        l_ref[...] = l_in[...]
        acc_ref[...] = acc_in[...]

    def one(kv_ref, b, diagonal):
        k = kv_ref[b, :BLOCK, :]
        v = kv_ref[b, BLOCK:, :]
        score = dot(q_ref[...], k, NT) * SCALE
        if diagonal:
            row = lax.broadcasted_iota(jnp.int32, (BLOCK, BLOCK), 0)
            col = lax.broadcasted_iota(jnp.int32, (BLOCK, BLOCK), 1)
            score = jnp.where(col <= row, score, -1e30)
        m_old = m_ref[...]
        m_new = jnp.maximum(m_old, jnp.max(score, axis=1, keepdims=True))
        weight = jnp.exp2(score - m_new[:, :1])
        shrink = jnp.exp2(m_old - m_new)
        l_ref[...] = l_ref[...] * shrink + (weight[:, :128] + weight[:, 128:])
        acc_ref[...] = acc_ref[...] * shrink + dot(weight.astype(BF16), v)
        m_ref[...] = m_new

    at = 0
    for kv_ref, count in zip(kv_refs, counts):
        for b in range(count):
            if first and at == 0:
                one(kv_ref, b, True)
            else:
                pl.when(flags[at] > 0)(functools.partial(one, kv_ref, b, False))
            at += 1
    if last:
        total = jnp.sum(l_ref[...], axis=1, keepdims=True)
        out_ref[...] = (acc_ref[...] / total).astype(BF16)


def attend(queries, kvs, flags, carry, last):
    first = carry is None
    counts = tuple(kv.shape[0] for kv in kvs)
    per_head = pl.BlockSpec((None, BLOCK, DH), lambda h, f: (h, 0, 0))
    columns = pl.BlockSpec((BLOCK, DH), lambda h, f: (0, h))
    carried = [jax.ShapeDtypeStruct((8, BLOCK, DH), F32)] * 3
    blocks = sum(counts)
    work = blocks * 8 * BLOCK * BLOCK
    kernel = functools.partial(attend_kernel, counts, first, last)
    return pl.pallas_call(
        kernel,
        grid_spec=pltpu.PrefetchScalarGridSpec(
            num_scalar_prefetch=1,
            grid=(8,),
            in_specs=[columns]
            + [pl.BlockSpec(kv.shape, lambda h, f: (0, 0, 0)) for kv in kvs]
            + ([] if first else [per_head] * 3),
            out_specs=columns if last else [per_head] * 3,
            scratch_shapes=[pltpu.VMEM((BLOCK, DH), F32)] * 3 if last else [],
        ),
        out_shape=jax.ShapeDtypeStruct((BLOCK, 8 * DH), BF16) if last else carried,
        compiler_params=pltpu.CompilerParams(vmem_limit_bytes=32 * 2**20),
        cost_estimate=pl.CostEstimate(
            flops=4 * work * DH, bytes_accessed=blocks * 2**17 + 6 * 2**20, transcendentals=work
        ),
        name="attend",
    )(flags, queries, *kvs, *(() if first else carry))


def call(kernel, outs, cost, *args):
    return pl.pallas_call(
        kernel,
        out_shape=outs,
        compiler_params=pltpu.CompilerParams(vmem_limit_bytes=48 * 2**20),
        cost_estimate=pl.CostEstimate(flops=cost, bytes_accessed=3 * 2**20, transcendentals=2**20),
    )(*args)


def z_pairs(d):
    return [(x * ZS + z, x * ZS + (z + d) % ZS) for x in range(XS) for z in range(ZS)]


def x_pairs(d):
    return [(x * ZS + z, (x + d) % XS * ZS + z) for x in range(XS) for z in range(ZS)]


def z_send(a, d):
    return lax.ppermute(a, "ctx", z_pairs(d))


def x_send(a, d):
    return lax.ppermute(a, "ctx", x_pairs(d))


def per_device(
    ssm_input,
    gate_input,
    in_state,
    out_state,
    step_size,
    log_decay,
    skip_gain,
    norm_gain,
    queries,
    keys,
    values,
):
    place = lax.axis_index("ctx")
    x, z = place // ZS, place % ZS
    rows = jnp.stack([x, (x + 3) % XS, (x + 1) % XS, (x + 2) % XS])

    def seen(d):
        return (rows * ZS + (z + d) % ZS < place).astype(jnp.int32)

    kv = jnp.concatenate([keys, values], axis=0)
    column = jnp.stack([kv, x_send(kv, 1), x_send(kv, -1), x_send(kv, 2)])

    struct = jax.ShapeDtypeStruct
    y, msg, ec = call(
        local_kernel,
        [
            struct((BLOCK, WIDTH), F32),
            struct((CTX, 48, 128), BF16),
            struct((BLOCK, HEADS), F32),
        ],
        500_000_000,
        ssm_input,
        in_state,
        out_state,
        step_size,
        log_decay,
        skip_gain.reshape(1, HEADS),
    )
    msg = lax.all_to_all(msg, "ctx", 0, 0)
    state = call(scan_kernel, struct((CTX, 32, 128), BF16), 1_000_000, msg)
    state = lax.all_to_all(state, "ctx", 0, 0).reshape(8, 128, 128)
    gated, squares = call(
        gate_kernel,
        [struct((BLOCK, WIDTH), F32), struct((8, BLOCK), F32)],
        100_000_000,
        y,
        out_state,
        state,
        ec,
        gate_input,
    )
    squares = lax.all_gather(squares[0], "head")
    mamba_out = call(
        norm_kernel,
        struct((BLOCK, WIDTH), BF16),
        10_000_000,
        gated,
        squares,
        norm_gain.reshape(1, WIDTH),
    )

    carry = attend(queries, [column], seen(0), None, False)
    right = left = column
    for step in range(1, 4):
        right, left = z_send(right, 1), z_send(left, -1)
        flags = jnp.concatenate([seen(-step), seen(step)])
        carry = attend(queries, [right, left], flags, carry, False)
    right, left = z_send(right[:2], 1), z_send(left[2:], -1)
    attention_out = attend(queries, [right, left], seen(4), carry, True)
    return mamba_out, attention_out


def solution(mesh):
    both = P("ctx", "head")
    return jax.shard_map(
        per_device,
        mesh=mesh,
        in_specs=(both,) * 6 + (P("head"), P("head")) + (both,) * 3,
        out_specs=(both, both),
        check_vma=False,
    )
```

time: 399 us -> 221 us (0.55)
  Pallas kernels: 0 us -> 152 us
  matrix products: 131 us -> 0 us
  waiting for transfers between devices: 108 us -> 13.9 us
  local copies, waits for them, and re-layouts: 54.3 us -> 7.74 us
  blocking collectives: 45.1 us -> 14.8 us
  other arithmetic: 31.6 us -> 1.56 us
  starting transfers between devices: 0.11 us -> 29.2 us
  loops' own time: 12.9 us -> 0 us
  between operations: 13.9 us -> 1.08 us
    pallas_call x0 -> x9, Pallas kernels: none -> 152 us  [the longest x5 147 us: attend(): pl.pallas_call(kernel, grid_spec=pltpu.PrefetchScalarGridSpec(num_scalar_...]
    dot_general x36 -> x0, matrix products: 131 us -> none  [the longest x16 61 us: update(): jnp.einsum('gqtj,jgd->gqtd', weight.astype(jnp.bfloat16), value_block, pr...]
    all_gather x3 -> x0, waiting for transfers between devices: 106 us -> none  [the longest x1 77.7 us: attention(): value_piece = lax.all_gather(values, 'ctx', axis=0, tiled=True)]
    dynamic_slice x78 -> x0, local copies, waits for them, and re-layouts: 48.4 us -> none  [the longest x62 39 us: one(): lax.dynamic_index_in_dim(a, turn, 0, False).astype(own.dtype)]
    all_to_all x0 -> x2, starting transfers between devices: none -> 18.2 us  [the longest x1 10 us: per_device(): msg = lax.all_to_all(msg, 'ctx', 0, 0)]
    psum x1 -> x0, blocking collectives: 16.2 us -> none  [mamba_mixer(): squares = lax.psum(jnp.sum(gated * gated, axis=1), 'head')]
    reduce_sum x17 -> x0, other arithmetic: 15.6 us -> none  [the longest x16 14.1 us: update(): total_sum = total_sum * shrink + jnp.sum(weight, axis=-1)]
    all_gather x1, blocking collectives: 28.9 us -> 14.8 us  [per_device(): squares = lax.all_gather(squares[0], 'head')]
  transfers between devices with their start and end apart: 3 -> 13, of which waited for: 2 -> 4; matrix products, arithmetic and copies ran while one was open for 41% -> 1% of each run, Pallas kernels for 0% -> 60%
where the time goes in v1:
time: 221 us; the launch traced here: 220 us
  Pallas kernels  152 us (69%)
  starting transfers between devices  29.2 us (13%)
  blocking collectives  14.8 us (7%)
  waiting for transfers between devices  13.9 us (6%)
  local copies, waits for them, and re-layouts  7.74 us (4%)
    pallas_call x5, Pallas kernels, attend(): pl.pallas_call(kernel, grid_spec=pltpu.PrefetchScalarGridSpec(num_scalar_...  147 us
    all_gather x1, blocking collectives, per_device(): squares = lax.all_gather(squares[0], 'head')  14.8 us
    all_to_all x1, starting transfers between devices, per_device(): msg = lax.all_to_all(msg, 'ctx', 0, 0)  10 us
    all_to_all x1, starting transfers between devices, per_device(): state = lax.all_to_all(state, 'ctx', 0, 0).reshape(8, 128, 128)  8.13 us
    ppermute x8, starting transfers between devices, z_send(): return lax.ppermute(a, 'ctx', z_pairs(d))  7.77 us
    unnamed x49, local copies, waits for them, and re-layouts  7.69 us
    all_to_all x1, waiting for transfers between devices, per_device(): msg = lax.all_to_all(msg, 'ctx', 0, 0)  6.95 us
    ppermute x3, waiting for transfers between devices, x_send(): return lax.ppermute(a, 'ctx', x_pairs(d))  5.46 us
  transfers between devices with their start and end apart: 13, of which 4 were waited for; matrix products, arithmetic and copies ran while one was open for 1% of the time, Pallas kernels for 60%

profile of v1, /device:TPU:231, one launch (start us, length us, event | category | flops | bytes accessed | tf_op | source)
XLA Modules:
  0.0 220.0 jit_solution(12802435064094650435)
XLA Ops:
  0.6 0.9 constant_dynamic-update-slice_fusion.1
  3.0 1.8 collective-permute-start
  4.8 5.3 %collective-permute-done.1 = bf16[512,128]{1,0:T(8,128)(2,1)S(1)} collective-permute-done((bf16[512,128]{1,0:T(8,128)(2,1)S(1)}, bf16[512,128]{1,0:T(8,128)(2,1)S(1)}, u32[]{:S(2)}, u32[]{:S(2)}) %collective-permute-start.1) | collective-permute-done | bytes 131104 | tf_op jit(solution)/shard_map/ppermute | solution.py:222
  10.5 1.5 collective-permute-start.7
  12.9 2.2 shard_map.122
  15.1 10.0 %all-to-all-start = ((bf16[32,48,128]{2,1,0:T(8,128)(2,1)}), bf16[32,48,128]{2,1,0:T(8,128)(2,1)S(1)}, u32[]{:S(2)}, u32[]{:S(2)}) async-start(bf16[32,48,128]{2,1,0:T(8,128)(2,1)} %get-tuple-element.20), calls=%async_computation | async-start | bytes 786432 | tf_op jit(solution)/shard_map/all_to_all | solution.py:264
  25.7 1.2 collective-permute-start.8
  28.3 7.0 %all-to-all-done.msg_ref = bf16[32,48,128]{2,1,0:T(8,128)(2,1)S(1)} async-done(((bf16[32,48,128]{2,1,0:T(8,128)(2,1)}), bf16[32,48,128]{2,1,0:T(8,128)(2,1)S(1)}, u32[]{:S(2)}, u32[]{:S(2)}) %all-to-all-start) | async-done | bytes 393248 | tf_op jit(solution)/shard_map/all_to_all | solution.py:264
  36.1 8.1 %all-to-all-start.1 = ((bf16[32,32,128]{2,1,0:T(8,128)(2,1)}), bf16[32,32,128]{2,1,0:T(8,128)(2,1)S(1)}, u32[]{:S(2)}, u32[]{:S(2)}) async-start(bf16[32,32,128]{2,1,0:T(8,128)(2,1)} %shard_map.123), calls=%async_computation.1 | async-start | bytes 524288 | tf_op jit(solution)/shard_map/all_to_all | solution.py:266
  44.2 1.5 collective-permute-done.4.refs_1_
  45.7 1.9 collective-permute-start.5
  48.3 18.0 %attend.5 = (f32[8,256,128]{2,1,0:T(8,128)S(1)}, f32[8,256,128]{2,1,0:T(8,128)S(1)}, f32[8,256,128]{2,1,0:T(8,128)S(1)}) custom-call(s32[4]{0:T(128)S(1)} %get-tuple-element.36.flags, bf16[256,1024]{1,0:T(8,128)(2,1)S(1)} %copy-done, bf16[4,512,128]{2,1,0:T(8,128)(2,1)S(1)} %pad_maximum_fusion.refs_1_), custom_call_target="tpu_custom_call" | custom-call | flops 1073741824 | bytes 6815744 | tf_op jit(solution)/shard_map/attend/pallas_call | solution.py:180
  67.0 36.5 %attend.6 = (f32[8,256,128]{2,1,0:T(8,128)S(1)}, f32[8,256,128]{2,1,0:T(8,128)S(1)}, f32[8,256,128]{2,1,0:T(8,128)S(1)}) custom-call(s32[8]{0:T(128)S(1)} %copy-done.10, bf16[256,1024]{1,0:T(8,128)(2,1)S(1)} %copy-done, bf16[4,512,128]{2,1,0:T(8,128)(2,1)S(1)} %copy-done.6, bf16[4,512,128]{2,1,0:T(8,128)(2,1)} %collective-permute-done.7.refs_2_, ...), custom_call_target="tpu_custom_call" | custom-call | flops 2147483648 | bytes 7340032 | tf_op jit(solution)/shard_map/attend/pallas_call | solution.py:180
  103.5 36.6 %attend.7 = (f32[8,256,128]{2,1,0:T(8,128)S(1)}, f32[8,256,128]{2,1,0:T(8,128)S(1)}, f32[8,256,128]{2,1,0:T(8,128)S(1)}) custom-call(s32[8]{0:T(128)S(1)} %add_convert_fusion.1.flags, bf16[256,1024]{1,0:T(8,128)(2,1)S(1)} %copy-done, bf16[4,512,128]{2,1,0:T(8,128)(2,1)} %collective-permute-done.4.refs_1_, ...), custom_call_target="tpu_custom_call" | custom-call | flops 2147483648 | bytes 7340032 | tf_op jit(solution)/shard_map/attend/pallas_call | solution.py:180
  140.2 1.0 copy-done.11
  141.2 1.0 copy-done.13
  142.2 1.0 copy-done.15
  143.2 0.8 copy-done.3
  144.0 0.9 shard_map.124
  145.1 2.7 %collective-permute-start.6 = (bf16[2,512,128]{2,1,0:T(8,128)(2,1)S(1)}, bf16[2,512,128]{2,1,0:T(8,128)(2,1)S(1)}, u32[]{:S(2)}, u32[]{:S(2)}) collective-permute-start(bf16[2,512,128]{2,1,0:T(8,128)(2,1)S(1)} %slice.12), channel_id=1, source_target_pairs={{0,8},{8,16},{16,24},{24,32},{32,40},{40,48},{48,56},{56,0},{64,72... | collective-permute-start | bytes 786440 | tf_op jit(solution)/shard_map/ppermute | solution.py:218
  147.8 14.8 %all-gather = f32[8,1,256]{2,1,0:T(1,128)S(1)} all-gather(f32[1,1,256]{2,1,0:T(1,128)S(1)} %slice_bitcast_fusion), channel_id=1, replica_groups=mesh['ctx'=32,'head'=8] {'head'}, dimensions={0}, use_global_device_ids=true | all-gather | bytes 9216 | tf_op jit(solution)/shard_map/all_gather | solution.py:277
  163.3 1.2 shard_map.125
  164.5 35.6 %attend.8 = (f32[8,256,128]{2,1,0:T(8,128)S(1)}, f32[8,256,128]{2,1,0:T(8,128)S(1)}, f32[8,256,128]{2,1,0:T(8,128)S(1)}) custom-call(s32[8]{0:T(128)S(1)} %add_convert_fusion.flags, bf16[256,1024]{1,0:T(8,128)(2,1)S(1)} %copy-done, bf16[4,512,128]{2,1,0:T(8,128)(2,1)S(1)} %collective-permute-done.5.refs_1_, ...), custom_call_target="tpu_custom_call" | custom-call | flops 2147483648 | bytes 7340032 | tf_op jit(solution)/shard_map/attend/pallas_call | solution.py:180
  200.1 19.9 %attend.9 = bf16[256,1024]{1,0:T(8,128)(2,1)} custom-call(s32[4]{0:T(128)S(1)} %get-tuple-element.44.flags, bf16[256,1024]{1,0:T(8,128)(2,1)S(1)} %copy-done, bf16[2,512,128]{2,1,0:T(8,128)(2,1)S(1)} %collective-permute-done.6.refs_1_, bf16[2,512,128]{2,1,0:T(8,128)(2,1)S(1)} %collective-permute-done.10.refs_2_, ...), custom_call_target="tpu_custom_call" | custom-call | flops 1073741824 | bytes 6815744 | tf_op jit(solution)/shard_map/attend/pallas_call | solution.py:180
  (70 shorter events, 7.5 us)
Async XLA Ops:
  1.5 8.6 %collective-permute-start.1 = (bf16[512,128]{1,0:T(8,128)(2,1)S(1)}, bf16[512,128]{1,0:T(8,128)(2,1)S(1)}, u32[]{:S(2)}, u32[]{:S(2)}) collective-permute-start(bf16[512,128]{1,0:T(8,128)(2,1)S(1)} %constant_dynamic-update-slice_fusion), channel_id=1, source_target_pairs={{0,192},{8,200},{16,208},{24,216},{32,224},{40,232},{48,240},{56,2... | collective-permute-start | bytes 393224 | tf_op jit(solution)/shard_map/ppermute | solution.py:222
  2.2 8.0 %collective-permute-start.2 = (bf16[512,128]{1,0:T(8,128)(2,1)S(1)}, bf16[512,128]{1,0:T(8,128)(2,1)S(1)}, u32[]{:S(2)}, u32[]{:S(2)}) collective-permute-start(bf16[512,128]{1,0:T(8,128)(2,1)S(1)} %constant_dynamic-update-slice_fusion), channel_id=1, source_target_pairs={{0,128},{8,136},{16,144},{24,152},{32,160},{40,168},{48,176},{56,1... | collective-permute-start | bytes 393224 | tf_op jit(solution)/shard_map/ppermute | solution.py:222
  3.0 7.3 %collective-permute-start = (bf16[512,128]{1,0:T(8,128)(2,1)S(1)}, bf16[512,128]{1,0:T(8,128)(2,1)S(1)}, u32[]{:S(2)}, u32[]{:S(2)}) collective-permute-start(bf16[512,128]{1,0:T(8,128)(2,1)S(1)} %constant_dynamic-update-slice_fusion), channel_id=1, source_target_pairs={{0,64},{8,72},{16,80},{24,88},{32,96},{40,104},{48,112},{56,120},{... | collective-permute-start | bytes 393224 | tf_op jit(solution)/shard_map/ppermute | solution.py:222
  10.3 1.6 copy-start.18
  10.3 1.9 copy-start.4
  10.3 1.7 copy-start.19
  10.4 15.0 %collective-permute-start.3 = (bf16[4,512,128]{2,1,0:T(8,128)(2,1)S(1)}, bf16[4,512,128]{2,1,0:T(8,128)(2,1)S(1)}, u32[]{:S(2)}, u32[]{:S(2)}) collective-permute-start(bf16[4,512,128]{2,1,0:T(8,128)(2,1)S(1)} %pad_maximum_fusion.refs_1_), channel_id=1, source_target_pairs={{0,8},{8,16},{16,24},{24,32},{32,40},{40,48},{48,56},{56,0},{64,72... | collective-permute-start | bytes 1572872 | tf_op jit(solution)/shard_map/ppermute | solution.py:218
  10.5 15.2 %collective-permute-start.7 = (bf16[4,512,128]{2,1,0:T(8,128)(2,1)S(1)}, bf16[4,512,128]{2,1,0:T(8,128)(2,1)}, u32[]{:S(2)}, u32[]{:S(2)}) collective-permute-start(bf16[4,512,128]{2,1,0:T(8,128)(2,1)S(1)} %pad_maximum_fusion.refs_1_), channel_id=1, source_target_pairs={{0,56},{8,0},{16,8},{24,16},{32,24},{40,32},{48,40},{56,48},{64,12... | collective-permute-start | bytes 1572872 | tf_op jit(solution)/shard_map/ppermute | solution.py:218
  15.1 20.2 %all-to-all-start = ((bf16[32,48,128]{2,1,0:T(8,128)(2,1)}), bf16[32,48,128]{2,1,0:T(8,128)(2,1)S(1)}, u32[]{:S(2)}, u32[]{:S(2)}) async-start(bf16[32,48,128]{2,1,0:T(8,128)(2,1)} %get-tuple-element.20), calls=%async_computation | async-start | bytes 786432 | tf_op jit(solution)/shard_map/all_to_all | solution.py:264
  25.3 10.7 %copy-start.5 = (bf16[4,512,128]{2,1,0:T(8,128)(2,1)}, bf16[4,512,128]{2,1,0:T(8,128)(2,1)S(1)}, u32[]{:S(2)}) copy-start(bf16[4,512,128]{2,1,0:T(8,128)(2,1)S(1)} %collective-permute-done.3.refs_1_) | copy-start | bytes 1572868
  25.4 20.3 %collective-permute-start.4 = (bf16[4,512,128]{2,1,0:T(8,128)(2,1)S(1)}, bf16[4,512,128]{2,1,0:T(8,128)(2,1)}, u32[]{:S(2)}, u32[]{:S(2)}) collective-permute-start(bf16[4,512,128]{2,1,0:T(8,128)(2,1)S(1)} %collective-permute-done.3.refs_1_), channel_id=1, source_target_pairs={{0,8},{8,16},{16,24},{24,32},{32,40},{40,48},{48,56},{56,0},{64,72... | collective-permute-start | bytes 1572872 | tf_op jit(solution)/shard_map/ppermute | solution.py:218
  25.7 21.9 %collective-permute-start.8 = (bf16[4,512,128]{2,1,0:T(8,128)(2,1)}, bf16[4,512,128]{2,1,0:T(8,128)(2,1)}, u32[]{:S(2)}, u32[]{:S(2)}) collective-permute-start(bf16[4,512,128]{2,1,0:T(8,128)(2,1)} %collective-permute-done.7.refs_2_), channel_id=1, source_target_pairs={{0,56},{8,0},{16,8},{24,16},{32,24},{40,32},{48,40},{56,48},{64,12... | collective-permute-start | bytes 1572872 | tf_op jit(solution)/shard_map/ppermute | solution.py:218
  36.1 12.2 %copy-start = (bf16[256,1024]{1,0:T(8,128)(2,1)S(1)}, bf16[256,1024]{1,0:T(8,128)(2,1)}, u32[]{:S(2)}) copy-start(bf16[256,1024]{1,0:T(8,128)(2,1)} %refs_0_.9) | copy-start | bytes 1572868
  36.1 107.1 %all-to-all-start.1 = ((bf16[32,32,128]{2,1,0:T(8,128)(2,1)}), bf16[32,32,128]{2,1,0:T(8,128)(2,1)S(1)}, u32[]{:S(2)}, u32[]{:S(2)}) async-start(bf16[32,32,128]{2,1,0:T(8,128)(2,1)} %shard_map.123), calls=%async_computation.1 | async-start | bytes 524288 | tf_op jit(solution)/shard_map/all_to_all | solution.py:266
  45.7 99.4 %collective-permute-start.5 = (bf16[4,512,128]{2,1,0:T(8,128)(2,1)}, bf16[4,512,128]{2,1,0:T(8,128)(2,1)S(1)}, u32[]{:S(2)}, u32[]{:S(2)}) collective-permute-start(bf16[4,512,128]{2,1,0:T(8,128)(2,1)} %collective-permute-done.4.refs_1_), channel_id=1, source_target_pairs={{0,8},{8,16},{16,24},{24,32},{32,40},{40,48},{48,56},{56,0},{64,72... | collective-permute-start | bytes 1572872 | tf_op jit(solution)/shard_map/ppermute | solution.py:218
  47.5 97.4 %collective-permute-start.9 = (bf16[4,512,128]{2,1,0:T(8,128)(2,1)}, bf16[4,512,128]{2,1,0:T(8,128)(2,1)S(1)}, u32[]{:S(2)}, u32[]{:S(2)}) collective-permute-start(bf16[4,512,128]{2,1,0:T(8,128)(2,1)} %collective-permute-done.8.refs_2_), channel_id=1, source_target_pairs={{0,56},{8,0},{16,8},{24,16},{32,24},{40,32},{48,40},{56,48},{64,12... | collective-permute-start | bytes 1572872 | tf_op jit(solution)/shard_map/ppermute | solution.py:218
  48.3 18.0 %copy-start.6 = (bf16[4,512,128]{2,1,0:T(8,128)(2,1)S(1)}, bf16[4,512,128]{2,1,0:T(8,128)(2,1)}, u32[]{:S(2)}) copy-start(bf16[4,512,128]{2,1,0:T(8,128)(2,1)} %copy-done.5) | copy-start | bytes 1572868
  103.5 39.6 %copy-start.1 = (bf16[256,1024]{1,0:T(8,128)(2,1)S(1)}, bf16[256,1024]{1,0:T(8,128)(2,1)}, u32[]{:S(2)}) copy-start(bf16[256,1024]{1,0:T(8,128)(2,1)} %z_ref.1) | copy-start | bytes 1572868
  140.2 1.0 copy-start.11
  144.0 20.5 %copy-start.16 = (f32[8,256,128]{2,1,0:T(8,128)S(1)}, f32[8,256,128]{2,1,0:T(8,128)}, u32[]{:S(2)}) copy-start(f32[8,256,128]{2,1,0:T(8,128)} %copy-done.15) | copy-start | bytes 3145732
  144.9 19.6 %copy-start.12 = (f32[8,256,128]{2,1,0:T(8,128)S(1)}, f32[8,256,128]{2,1,0:T(8,128)}, u32[]{:S(2)}) copy-start(f32[8,256,128]{2,1,0:T(8,128)} %copy-done.11) | copy-start | bytes 3145732
  144.9 55.1 %collective-permute-start.10 = (bf16[2,512,128]{2,1,0:T(8,128)(2,1)S(1)}, bf16[2,512,128]{2,1,0:T(8,128)(2,1)S(1)}, u32[]{:S(2)}, u32[]{:S(2)}) collective-permute-start(bf16[2,512,128]{2,1,0:T(8,128)(2,1)S(1)} %slice.13), channel_id=1, source_target_pairs={{0,56},{8,0},{16,8},{24,16},{32,24},{40,32},{48,40},{56,48},{64,12... | collective-permute-start | bytes 786440 | tf_op jit(solution)/shard_map/ppermute | solution.py:218
  145.1 55.0 %collective-permute-start.6 = (bf16[2,512,128]{2,1,0:T(8,128)(2,1)S(1)}, bf16[2,512,128]{2,1,0:T(8,128)(2,1)S(1)}, u32[]{:S(2)}, u32[]{:S(2)}) collective-permute-start(bf16[2,512,128]{2,1,0:T(8,128)(2,1)S(1)} %slice.12), channel_id=1, source_target_pairs={{0,8},{8,16},{16,24},{24,32},{32,40},{40,48},{48,56},{56,0},{64,72... | collective-permute-start | bytes 786440 | tf_op jit(solution)/shard_map/ppermute | solution.py:218
  162.6 1.9 copy-start.14
  (11 other events, 8.9 us)
